TPU v7x, 32 devices: a whole 2x2x4 slice. The times are simulated.
32 devices in a mesh: grid: 16 (over z, x, core), col: 2 (over y).
Axes of the slice: x: 2, y: 2, z: 4, core: 2. Of those that a mesh axis runs over, the one named last changes fastest.
Arguments:
- density: bfloat16 [16384, 16384], P('grid', 'col'), may hold values from -0.5 to 0.5
- centres: float32 [3, 16384], replicated, may hold values from -0.4 to 0.4
- exponents: float32 [16384], replicated, may hold values from 2 to 16
- coords: float32 [64, 3, 256], P('grid'), may hold values from -0.4 to 0.4
- weights: float32 [64, 256], P('grid'), may hold values from 0.078125 to 0.78125
- core_density: float32 [64, 256], P('grid'), may hold values from 0.3 to 3
- counts: int32 [64], P('grid'), may hold values from 1 to 256, 4096 in all
- blocks: int32 [64, 2], replicated, may hold values from 0 to 127, as said below
Outputs:
- potential_matrix_xc: float32 [16384, 16384], P('grid', 'col')
- orbital_charge_samples: float32 [64, 256], P('grid')
- xc_batch_amounts: float32 [64], P('grid')
Inputs may be any that keep to these rules, and one draw needn't show every extreme that they name: Entry c of a batch's row names a block in the c-th of 2 equal runs of 64 blocks; for one grid index's 4 batches the values // 8 in one column c are distinct. The points in use are the first counts[b] slots.
All inputs are finite; a program needn't handle non-finite values. No bound on the sum of `counts` on one device may be relied on, other than what follows from the above.
Results may differ from a plain program's by a relative error of at most 0.0028.
Values may be sent and summed in bfloat16 or wider, within the bound.
A program may use at most 128 MiB of HBM per device.

v0:
```python
import math

import jax
import jax.numpy as jnp
from jax import lax
from jax.experimental import pallas as pl
from jax.experimental.pallas import tpu as pltpu
from jax.sharding import PartitionSpec as P

BLK = 128
FILL_ROWS = 32
FIRST_FILL = 0.5
GROUP = 4
VMEM_LIMIT = 64 * 1024 * 1024
MESH = pl.DeviceIdType.MESH
F32 = jnp.float32
BF16 = jnp.bfloat16

kappa_pbe = 0.804
mu_coef = 0.2195
slater = -0.7385587663820224
grad_scale = 4.0 * (3.0 * math.pi**2) ** (2.0 / 3.0)
soft_square = 0.25


def xc_kernel(total, grad_square):
    root = jnp.sqrt(total * total + soft_square)
    regular = 0.5 * (total + root)
    log_regular = jnp.log(regular)
    third = jnp.exp(log_regular * (1.0 / 3.0))
    four_thirds = jnp.exp(log_regular * (4.0 / 3.0))
    scaled = grad_scale * four_thirds * four_thirds
    inverse = 1.0 / (kappa_pbe * scaled + mu_coef * grad_square)
    ratio = scaled * inverse
    enhance = 1.0 + kappa_pbe - kappa_pbe * kappa_pbe * ratio
    energy = slater * four_thirds * enhance
    inner = (4.0 / 3.0) * enhance - (8.0 / 3.0) * kappa_pbe * kappa_pbe * ratio * (
        mu_coef * grad_square * inverse
    )
    deriv_density = slater * third * inner * (0.5 * (1.0 + total / root))
    deriv_sigma = slater * four_thirds * (kappa_pbe * kappa_pbe * mu_coef) * ratio * inverse
    return energy, deriv_density, deriv_sigma


def parts_of(value):
    first = value.astype(BF16).astype(F32)
    rest = value - first
    second = rest.astype(BF16).astype(F32)
    return first, second, rest - second


def outer_sum(left, right):
    l1, l2, l3 = parts_of(left)
    r1, r2, r3 = parts_of(right)
    lefts = jnp.concatenate([l1, l1, l1, l2, l2, l3], axis=0).astype(BF16)
    rights = jnp.concatenate([r1, r2, r3, r1, r2, r1], axis=0).astype(BF16)
    return lax.dot_general(
        lefts, rights, (((0,), (0,)), ((), ())), preferred_element_type=F32
    )


def batch_of(blocks_ref, requester, entry, owner, batches, row_blocks):
    found = jnp.int32(-1)
    for batch in range(batches):
        offset = blocks_ref[entry, requester * batches + batch] - owner * row_blocks
        found = jnp.where((offset >= 0) & (offset < row_blocks), batch, found)
    return found


def owners_of(sizes, blocks_ref, requester):
    grid_size, col_size, batches, row_blocks, halves = sizes
    return [
        [lax.div(blocks_ref[entry, requester * batches + batch], row_blocks) for batch in range(batches)]
        for entry in range(col_size)
    ]


def asked_batch(sizes, owners, owner):
    grid_size, col_size, batches, row_blocks, halves = sizes
    found = jnp.int32(0)
    for batch in range(1, batches):
        found = jnp.where(owners[owner // (grid_size // col_size)][batch] == owner, batch, found)
    return found


def fetch(pairs, sems):
    copies = [
        pltpu.make_async_copy(source, target, sems.at[place])
        for place, (source, target) in enumerate(pairs)
    ]
    for copy in copies:
        copy.start()
    return copies


def exchange_points(
    sizes,
    blocks_hbm,
    counts_hbm,
    coords_hbm,
    out_ref,
    blocks_ref,
    counts_ref,
    coords_ref,
    packed,
    staged,
    fetch_sem,
    own_sem,
    send,
    recv,
):
    grid_size, col_size, batches, row_blocks, halves = sizes
    me, col = lax.axis_index("grid"), lax.axis_index("col")
    fetched = fetch(
        [(blocks_hbm, blocks_ref), (counts_hbm, counts_ref), (coords_hbm, coords_ref)], fetch_sem
    )
    barrier = pltpu.get_barrier_semaphore()
    for step in range(1, grid_size):
        other = lax.rem(me + step, grid_size)
        pl.semaphore_signal(barrier, inc=1, device_id=(other, col), device_id_type=MESH)
    for copy in fetched:
        copy.wait()
    points = coords_ref[...]
    for batch in range(batches):
        count = jnp.full((1, BLK), counts_ref[batch].astype(F32), F32)
        pieces = []
        for half in range(halves):
            lanes = slice(half * BLK, (half + 1) * BLK)
            pieces += [points[d, batch : batch + 1, lanes] for d in range(3)] + [count]
        packed[batch] = jnp.concatenate(pieces, axis=0)
    owners = owners_of(sizes, blocks_ref, me)
    for owner in range(grid_size):
        staged[owner] = packed[asked_batch(sizes, owners, owner)]
    pl.semaphore_wait(barrier, grid_size - 1)
    copies = []
    for step in range(1, grid_size):
        other = lax.rem(me + step, grid_size)
        copy = pltpu.make_async_remote_copy(
            src_ref=staged.at[other],
            dst_ref=out_ref.at[me],
            send_sem=send.at[step],
            recv_sem=recv.at[step],
            device_id=(other, col),
            device_id_type=MESH,
        )
        copy.start()
        copies.append(copy)
    own = pltpu.make_async_copy(staged.at[me], out_ref.at[me], own_sem)
    own.start()
    for copy in copies:
        copy.wait()
    own.wait()


def exchange_sums(
    sizes,
    blocks_hbm,
    counts_hbm,
    weights_hbm,
    core_hbm,
    sums_hbm,
    out_ref,
    extra_ref,
    sums_ref,
    blocks_ref,
    counts_ref,
    weights_ref,
    core_ref,
    fetch_sem,
    landed,
    col_sums,
    fields,
    staged,
    extra,
    own_sem,
    send_a,
    recv_a,
    send_b,
    recv_b,
    send_c,
    recv_c,
):
    grid_size, col_size, batches, row_blocks, halves = sizes
    me, col = lax.axis_index("grid"), lax.axis_index("col")
    fetched = fetch(
        [
            (blocks_hbm, blocks_ref),
            (counts_hbm, counts_ref),
            (weights_hbm, weights_ref),
            (core_hbm, core_ref),
            (sums_hbm, sums_ref),
        ],
        fetch_sem,
    )
    barrier = pltpu.get_barrier_semaphore()
    for step in range(1, grid_size):
        other = lax.rem(me + step, grid_size)
        pl.semaphore_signal(barrier, inc=1, device_id=(other, col), device_id_type=MESH)
    for step in range(1, col_size):
        other = lax.rem(col + step, col_size)
        pl.semaphore_signal(barrier, inc=1, device_id=(me, other), device_id_type=MESH)
    for copy in fetched:
        copy.wait()
    owners = owners_of(sizes, blocks_ref, me)
    asked = [asked_batch(sizes, owners, owner) for owner in range(grid_size)]
    pl.semaphore_wait(barrier, grid_size + col_size - 2)

    copies = []
    for step in range(1, grid_size):
        other = lax.rem(me + step, grid_size)
        copy = pltpu.make_async_remote_copy(
            src_ref=sums_ref.at[other],
            dst_ref=landed.at[me],
            send_sem=send_a.at[step],
            recv_sem=recv_a.at[step],
            device_id=(other, col),
            device_id_type=MESH,
        )
        copy.start()
        copies.append(copy)
    kept = fetch([(sums_ref.at[me], landed.at[me])], own_sem)
    for copy in copies:
        copy.wait()
    kept[0].wait()

    for batch in range(batches):
        total = None
        for entry in range(col_size):
            term = landed[owners[entry][batch]]
            total = term if total is None else total + term
        col_sums[col, batch] = total
    copies = []
    for step in range(1, col_size):
        other = lax.rem(col + step, col_size)
        copy = pltpu.make_async_remote_copy(
            src_ref=col_sums.at[col],
            dst_ref=col_sums.at[col],
            send_sem=send_b.at[step],
            recv_sem=recv_b.at[step],
            device_id=(me, other),
            device_id_type=MESH,
        )
        copy.start()
        copies.append(copy)
    for copy in copies:
        copy.wait()
    summed = col_sums[0]
    for entry in range(1, col_size):
        summed = summed + col_sums[entry]

    places = [(batch, half) for batch in range(batches) for half in range(halves)]

    def rows_of(field):
        return jnp.concatenate(
            [summed[batch, 4 * half + field : 4 * half + field + 1] for batch, half in places],
            axis=0,
        )

    def rows_in(ref):
        value = ref[...]
        return jnp.concatenate(
            [value[batch : batch + 1, half * BLK : (half + 1) * BLK] for batch, half in places],
            axis=0,
        )

    lanes = lax.broadcasted_iota(jnp.int32, (1, BLK), 1)
    live = jnp.concatenate(
        [jnp.where(lanes + half * BLK < counts_ref[batch], 1.0, 0.0) for batch, half in places],
        axis=0,
    )
    valence = jnp.where(live > 0.0, rows_of(0), 0.0)
    gradient = [jnp.where(live > 0.0, rows_of(1 + d), 0.0) for d in range(3)]
    grad_square = (
        gradient[0] * gradient[0] + gradient[1] * gradient[1] + gradient[2] * gradient[2]
    )
    energy, deriv_density, deriv_sigma = xc_kernel(valence + rows_in(core_ref), grad_square)
    point_scale = rows_in(weights_ref) * live
    spread = 2.0 * point_scale * deriv_sigma
    table = [point_scale * deriv_density] + [spread * gradient[d] for d in range(3)]
    for batch in range(batches):
        fields[batch] = jnp.concatenate(
            [
                table[k][batch * halves + half : batch * halves + half + 1]
                for half in range(halves)
                for k in range(4)
            ],
            axis=0,
        )
    for owner in range(grid_size):
        staged[owner] = fields[asked[owner]]
    copies = []
    for step in range(1, grid_size):
        other = lax.rem(me + step, grid_size)
        copy = pltpu.make_async_remote_copy(
            src_ref=staged.at[other],
            dst_ref=out_ref.at[me],
            send_sem=send_c.at[step],
            recv_sem=recv_c.at[step],
            device_id=(other, col),
            device_id_type=MESH,
        )
        copy.start()
        copies.append(copy)
    extra[0] = valence
    extra[1] = point_scale * energy
    kept = fetch([(staged.at[me], out_ref.at[me]), (extra, extra_ref)], own_sem)
    for copy in copies:
        copy.wait()
    for copy in kept:
        copy.wait()


def list_tiles(sizes, blocks_ref, points_ref, tile_slot, tile_row, tile_col, item_tile, item_half):
    grid_size, col_size, batches, row_blocks, halves = sizes
    me, col = lax.axis_index("grid"), lax.axis_index("col")
    entry = lax.div(me, grid_size // col_size)

    def step(slot, carry):
        tiles, items = carry
        found = batch_of(blocks_ref, slot, entry, me, batches, row_blocks)
        batch = jnp.maximum(found, 0)
        has = found >= 0
        tile_slot[tiles] = slot
        tile_row[tiles] = blocks_ref[entry, slot * batches + batch]
        tile_col[tiles] = blocks_ref[col, slot * batches + batch]
        count = points_ref[slot, 3, 0]
        for half in range(halves):
            item_tile[items] = tiles
            item_half[items] = half
            items = items + jnp.where(has & (count > half * BLK), 1, 0)
        return tiles + jnp.where(has, 1, 0), items

    return lax.fori_loop(0, grid_size, step, (jnp.int32(0), jnp.int32(0)), unroll=True)


def half_rows(value, half, halves):
    picked = value[0:4]
    for other in range(1, halves):
        picked = jnp.where(half == other, value[4 * other : 4 * other + 4], picked)
    return picked


def functions_of(centres_ref, exponents_ref, row, column):
    rate = jnp.concatenate(
        [exponents_ref[pl.ds(row, 1), :], exponents_ref[pl.ds(column, 1), :]], axis=1
    )
    centre = jnp.concatenate(
        [
            centres_ref[:, pl.ds(pl.multiple_of(row * BLK, BLK), BLK)],
            centres_ref[:, pl.ds(pl.multiple_of(column * BLK, BLK), BLK)],
        ],
        axis=1,
    )
    return rate, centre


def distance_factors(points, rate, centre):
    square = jnp.sum(points * points, axis=0, keepdims=True)
    right = jnp.concatenate(
        [square, points, jnp.ones((1, BLK), F32), jnp.zeros((3, BLK), F32)], axis=0
    )
    left = jnp.concatenate(
        [
            -rate,
            2.0 * rate * centre,
            -rate * jnp.sum(centre * centre, axis=0, keepdims=True),
            jnp.zeros((3, 2 * BLK), F32),
        ],
        axis=0,
    )
    return right, left


def coefficients(rate, centre):
    lanes = lax.broadcasted_iota(jnp.int32, (1, 2 * BLK), 1)
    return jnp.concatenate(
        [
            rate,
            rate * centre,
            jnp.where(lanes >= BLK, 1.0, 0.0),
            jnp.zeros((3, 2 * BLK), F32),
        ],
        axis=0,
    )


def density_tiles(
    sizes,
    fills,
    blocks_hbm,
    density_ref,
    centres_hbm,
    exponents_hbm,
    points_hbm,
    sums_ref,
    matrix_ref,
    points_ref,
    blocks_ref,
    centres_ref,
    exponents_ref,
    fetch_sem,
    held,
    zeros,
    tile_slot,
    tile_row,
    tile_col,
    item_tile,
    item_half,
    tile_sem,
    fill_sem,
):
    grid_size, col_size, batches, row_blocks, halves = sizes
    col_blocks = density_ref.shape[1] // BLK
    first_row = lax.axis_index("grid") * row_blocks
    first_col = lax.axis_index("col") * col_blocks

    def tile_copy(tile):
        row = pl.multiple_of((tile_row[tile] - first_row) * BLK, BLK)
        column = pl.multiple_of((tile_col[tile] - first_col) * BLK, BLK)
        return pltpu.make_async_copy(
            density_ref.at[pl.ds(row, BLK), pl.ds(column, BLK)], held.at[tile], tile_sem.at[tile]
        )

    def fill_copy(index):
        return pltpu.make_async_copy(
            zeros, matrix_ref.at[pl.ds(index * FILL_ROWS, FILL_ROWS), :], fill_sem.at[index]
        )

    fetched = fetch(
        [
            (blocks_hbm, blocks_ref),
            (points_hbm, points_ref),
            (centres_hbm, centres_ref),
            (exponents_hbm, exponents_ref),
        ],
        fetch_sem,
    )
    zeros[...] = jnp.zeros_like(zeros)
    for index in range(fills):
        fill_copy(index).start()
    sums_ref[...] = jnp.zeros_like(sums_ref)
    fetched[0].wait()
    fetched[1].wait()
    tiles, items = list_tiles(
        sizes, blocks_ref, points_ref, tile_slot, tile_row, tile_col, item_tile, item_half
    )

    @pl.loop(0, tiles)
    def _(tile):
        tile_copy(tile).start()

    fetched[2].wait()
    fetched[3].wait()

    @pl.loop(0, tiles)
    def _(tile):
        tile_copy(tile).wait()

    def one(item):
        tile, half = item_tile[item], item_half[item]
        slot = tile_slot[tile]
        points = half_rows(points_ref[slot], half, halves)[0:3]
        rate, centre = functions_of(centres_ref, exponents_ref, tile_row[tile], tile_col[tile])
        right, left = distance_factors(points, rate, centre)
        value = jnp.exp(outer_sum(right, left))
        low = value.astype(BF16)
        panel = held[tile]
        left_sum = lax.dot_general(
            low[:, BLK:], panel, (((1,), (1,)), ((), ())), preferred_element_type=F32
        )
        right_sum = jnp.dot(low[:, :BLK], panel, preferred_element_type=F32)
        product = value * jnp.concatenate([left_sum, right_sum], axis=1)
        upper = product.astype(BF16)
        lower = (product - upper.astype(F32)).astype(BF16)
        c1, c2, c3 = parts_of(coefficients(rate, centre))
        rest = jnp.zeros((BLK - 24, 2 * BLK), F32)
        for_upper = jnp.concatenate([c1, c2, c3, rest], axis=0).astype(BF16)
        for_lower = jnp.concatenate([jnp.zeros_like(c1), c1, c2, rest], axis=0).astype(BF16)
        contract = (((1,), (1,)), ((), ()))
        terms = lax.dot_general(upper, for_upper, contract, preferred_element_type=F32)
        terms += lax.dot_general(lower, for_lower, contract, preferred_element_type=F32)
        terms = terms.T
        summed = terms[0:8] + terms[8:16] + terms[16:24]
        gradient = 2.0 * (summed[1:4] - points * summed[0:1])
        piece = jnp.concatenate([summed[4:5], gradient], axis=0)
        rows = lax.broadcasted_iota(jnp.int32, (4 * halves, BLK), 0)
        return slot, (rows >= 4 * half) & (rows < 4 * half + 4), jnp.concatenate([piece] * halves, 0)

    @pl.loop(0, lax.div(items + GROUP - 1, GROUP))
    def _(group):
        results = [one(jnp.minimum(GROUP * group + k, items - 1)) for k in range(GROUP)]
        for slot, chosen, piece in results:
            sums_ref[slot] = jnp.where(chosen, piece, sums_ref[slot])

    for index in range(fills):
        fill_copy(index).wait()


def potential_tiles(
    sizes,
    fills,
    blocks_hbm,
    centres_hbm,
    exponents_hbm,
    points_hbm,
    fields_hbm,
    extra_hbm,
    given_ref,
    matrix_ref,
    samples_ref,
    amounts_ref,
    fields_ref,
    extra_ref,
    points_ref,
    blocks_ref,
    centres_ref,
    exponents_ref,
    fetch_sem,
    total,
    zeros,
    tile_slot,
    tile_row,
    tile_col,
    item_tile,
    item_half,
    tile_goal,
    tile_sem,
    fill_sem,
):
    grid_size, col_size, batches, row_blocks, halves = sizes
    row_count, col_count = matrix_ref.shape
    first_row = lax.axis_index("grid") * row_blocks
    first_col = lax.axis_index("col") * (col_count // BLK)

    def fill_copy(index):
        return pltpu.make_async_copy(
            zeros, matrix_ref.at[pl.ds(index * FILL_ROWS, FILL_ROWS), :], fill_sem.at[index]
        )

    fetched = fetch(
        [
            (blocks_hbm, blocks_ref),
            (points_hbm, points_ref),
            (centres_hbm, centres_ref),
            (exponents_hbm, exponents_ref),
            (fields_hbm, fields_ref),
            (extra_hbm, extra_ref),
        ],
        fetch_sem,
    )
    zeros[...] = jnp.zeros_like(zeros)
    every_fill = range(fills, row_count // FILL_ROWS)
    for index in every_fill:
        fill_copy(index).start()
    fetched[0].wait()
    fetched[1].wait()
    tiles, items = list_tiles(
        sizes, blocks_ref, points_ref, tile_slot, tile_row, tile_col, item_tile, item_half
    )
    total[...] = jnp.zeros_like(total)
    for copy in fetched[2:]:
        copy.wait()

    @pl.loop(0, tiles)
    def _(tile):
        def step(k, goal):
            other = tile - 1 - k
            same = (tile_row[other] == tile_row[tile]) & (tile_col[other] == tile_col[tile])
            return jnp.where(same, other, goal)

        tile_goal[tile] = lax.fori_loop(0, tile, step, tile)

    for batch in range(batches):
        for half in range(halves):
            place = batch * halves + half
            samples_ref[batch : batch + 1, half * BLK : (half + 1) * BLK] = extra_ref[
                0, place : place + 1, :
            ]
        amounts_ref[batch] = jnp.sum(extra_ref[1, batch * halves : (batch + 1) * halves, :])

    def one(item):
        tile, half = item_tile[item], item_half[item]
        slot = tile_slot[tile]
        points = half_rows(points_ref[slot], half, halves)[0:3]
        field = half_rows(fields_ref[slot], half, halves)
        rate, centre = functions_of(centres_ref, exponents_ref, tile_row[tile], tile_col[tile])
        distance_right, distance_left = distance_factors(points, rate, centre)
        value = jnp.exp(outer_sum(distance_left, distance_right))
        slant = -2.0 * jnp.sum(field[1:4] * points, axis=0, keepdims=True)
        right = jnp.concatenate(
            [slant, 2.0 * field[1:4], field[0:1], jnp.zeros((3, BLK), F32)], axis=0
        )
        weighted = (value * outer_sum(coefficients(rate, centre), right)).astype(BF16)
        low = value.astype(BF16)
        left_side = jnp.concatenate([low[:BLK], weighted[:BLK]], axis=1)
        right_side = jnp.concatenate([weighted[BLK:], low[BLK:]], axis=1)
        return tile, lax.dot_general(
            left_side, right_side, (((1,), (1,)), ((), ())), preferred_element_type=F32
        )

    @pl.loop(0, lax.div(items + GROUP - 1, GROUP))
    def _(group):
        results = [one(jnp.minimum(GROUP * group + k, items - 1)) for k in range(GROUP)]
        for k, (tile, result) in enumerate(results):
            goal = jnp.where(GROUP * group + k < items, tile_goal[tile], grid_size)
            total[goal] += result

    for index in every_fill:
        fill_copy(index).wait()

    def tile_copy(tile):
        row = pl.multiple_of((tile_row[tile] - first_row) * BLK, BLK)
        column = pl.multiple_of((tile_col[tile] - first_col) * BLK, BLK)
        return pltpu.make_async_copy(
            total.at[tile], matrix_ref.at[pl.ds(row, BLK), pl.ds(column, BLK)], tile_sem.at[tile]
        )

    @pl.loop(0, tiles)
    def _(tile):
        @pl.when(tile_goal[tile] == tile)
        def _():
            tile_copy(tile).start()

    @pl.loop(0, tiles)
    def _(tile):
        @pl.when(tile_goal[tile] == tile)
        def _():
            tile_copy(tile).wait()


def local(density, centres, exponents, coords, weights, core_density, counts, blocks):
    grid_size = lax.axis_size("grid")
    col_size = lax.axis_size("col")
    row_count, col_count = density.shape
    batches, _, points_len = coords.shape
    row_blocks = row_count // BLK
    halves = points_len // BLK
    sizes = (grid_size, col_size, batches, row_blocks, halves)
    rates = exponents.reshape(exponents.shape[0] // BLK, BLK)
    table = blocks.T
    parts_first = coords.transpose(1, 0, 2)
    vmem = pl.BlockSpec(memory_space=pltpu.VMEM)
    smem = pl.BlockSpec(memory_space=pltpu.SMEM)
    anywhere = pl.BlockSpec(memory_space=pl.ANY)
    slot_shape = (grid_size, 4 * halves, BLK)
    hbm = pl.BlockSpec(memory_space=pltpu.HBM)
    table_memory = pltpu.SMEM(table.shape, jnp.int32)
    count_memory = pltpu.SMEM((batches,), jnp.int32)
    function_memory = [
        pltpu.VMEM(slot_shape, F32),
        table_memory,
        pltpu.VMEM(centres.shape, F32),
        pltpu.VMEM(rates.shape, F32),
        pltpu.SemaphoreType.DMA((6,)),
    ]
    slots = jax.ShapeDtypeStruct(slot_shape, F32)
    matrix = jax.ShapeDtypeStruct((row_count, col_count), F32)
    all_fills = row_count // FILL_ROWS
    fills = int(all_fills * FIRST_FILL)

    points = pl.pallas_call(
        lambda *refs: exchange_points(sizes, *refs),
        out_shape=slots,
        in_specs=[hbm, hbm, hbm],
        out_specs=anywhere,
        scratch_shapes=[
            table_memory,
            count_memory,
            pltpu.VMEM(parts_first.shape, F32),
            pltpu.VMEM((batches, 4 * halves, BLK), F32),
            pltpu.VMEM(slot_shape, F32),
            pltpu.SemaphoreType.DMA((3,)),
            pltpu.SemaphoreType.DMA,
            pltpu.SemaphoreType.DMA((grid_size,)),
            pltpu.SemaphoreType.DMA((grid_size,)),
        ],
        compiler_params=pltpu.CompilerParams(
            collective_id=0, has_side_effects=True, vmem_limit_bytes=VMEM_LIMIT
        ),
        name="exchange_points",
    )(table, counts, parts_first)

    lists = [pltpu.SMEM((grid_size + 1,), jnp.int32)] * 3 + [
        pltpu.SMEM((halves * grid_size + 1,), jnp.int32)
    ] * 2
    sums, started = pl.pallas_call(
        lambda *refs: density_tiles(sizes, fills, *refs),
        out_shape=(slots, matrix),
        in_specs=[hbm] * 5,
        out_specs=(vmem, anywhere),
        scratch_shapes=[
            *function_memory,
            pltpu.VMEM((grid_size, BLK, BLK), BF16),
            pltpu.VMEM((FILL_ROWS, col_count), F32),
            *lists,
            pltpu.SemaphoreType.DMA((grid_size,)),
            pltpu.SemaphoreType.DMA((all_fills,)),
        ],
        compiler_params=pltpu.CompilerParams(vmem_limit_bytes=VMEM_LIMIT),
        name="density_tiles",
    )(table, density, centres, rates, points)

    fields, extra = pl.pallas_call(
        lambda *refs: exchange_sums(sizes, *refs),
        out_shape=(slots, jax.ShapeDtypeStruct((2, batches * halves, BLK), F32)),
        in_specs=[hbm, hbm, hbm, hbm, hbm],
        out_specs=(anywhere, anywhere),
        scratch_shapes=[
            pltpu.VMEM(slot_shape, F32),
            table_memory,
            count_memory,
            pltpu.VMEM(weights.shape, F32),
            pltpu.VMEM(core_density.shape, F32),
            pltpu.SemaphoreType.DMA((5,)),
            pltpu.VMEM(slot_shape, F32),
            pltpu.VMEM((col_size, batches, 4 * halves, BLK), F32),
            pltpu.VMEM((batches, 4 * halves, BLK), F32),
            pltpu.VMEM(slot_shape, F32),
            pltpu.VMEM((2, batches * halves, BLK), F32),
            pltpu.SemaphoreType.DMA((2,)),
            pltpu.SemaphoreType.DMA((grid_size,)),
            pltpu.SemaphoreType.DMA((grid_size,)),
            pltpu.SemaphoreType.DMA((col_size,)),
            pltpu.SemaphoreType.DMA((col_size,)),
            pltpu.SemaphoreType.DMA((grid_size,)),
            pltpu.SemaphoreType.DMA((grid_size,)),
        ],
        compiler_params=pltpu.CompilerParams(
            collective_id=1, has_side_effects=True, vmem_limit_bytes=VMEM_LIMIT
        ),
        name="exchange_sums",
    )(table, counts, weights, core_density, sums)

    return pl.pallas_call(
        lambda *refs: potential_tiles(sizes, fills, *refs),
        out_shape=(
            matrix,
            jax.ShapeDtypeStruct((batches, points_len), F32),
            jax.ShapeDtypeStruct((batches,), F32),
        ),
        in_specs=[hbm] * 6 + [anywhere],
        out_specs=(anywhere, vmem, smem),
        scratch_shapes=[
            pltpu.VMEM(slot_shape, F32),
            pltpu.VMEM((2, batches * halves, BLK), F32),
            *function_memory,
            pltpu.VMEM((grid_size + 1, BLK, BLK), F32),
            pltpu.VMEM((FILL_ROWS, col_count), F32),
            *lists,
            pltpu.SMEM((grid_size + 1,), jnp.int32),
            pltpu.SemaphoreType.DMA((grid_size,)),
            pltpu.SemaphoreType.DMA((all_fills,)),
        ],
        input_output_aliases={6: 0},
        compiler_params=pltpu.CompilerParams(vmem_limit_bytes=VMEM_LIMIT),
        name="potential_tiles",
    )(table, centres, rates, points, fields, extra, started)


def solution(mesh):
    return jax.shard_map(
        local,
        mesh=mesh,
        in_specs=(
            P("grid", "col"),
            P(),
            P(),
            P("grid", None, None),
            P("grid", None),
            P("grid", None),
            P("grid"),
            P(),
        ),
        out_specs=(P("grid", "col"), P("grid", None), P("grid")),
        check_vma=False,
    )
```

profile of v0, /device:TPU:0, one launch (start us, length us, event | category | flops | bytes accessed | tf_op | source)
XLA Modules:
  0.0 41.0 jit_solution(13954656314585540257)
XLA Ops:
  0.6 9.1 %exchange_points.1.refs_4_.refs_3_ = f32[16,8,128]{2,1,0:T(8,128)} custom-call(s32[2,64]{1,0:T(2,128)} %bitcast.5, s32[4]{0:T(128)} %refs_1_.6, f32[3,4,256]{2,1,0:T(4,128)} %bitcast.9), custom_call_target="tpu_custom_call" | custom-call | tf_op jit(solution)/shard_map/exchange_points/pallas_call | solution.py:661
  9.7 7.0 %density_tiles.1 = (f32[16,8,128]{2,1,0:T(8,128)}, f32[1024,8192]{1,0:T(8,128)}) custom-call(s32[2,64]{1,0:T(2,128)} %bitcast.6, bf16[1024,8192]{1,0:T(8,128)(2,1)} %refs_1_.5, f32[3,16384]{1,0:T(4,128)} %refs_1_.7, f32[128,128]{1,0:T(8,128)} %bitcast.3, f32[16,8,128]{2,1,0:T(8,128)} %exchange_points.1.refs_4_.refs_3_), custom_call_target="tpu_custom_call" | custom-call | tf_op jit(solution)/shard_map/density_tiles/pallas_call | solution.py:686
  16.7 16.6 %exchange_sums.1 = (f32[16,8,128]{2,1,0:T(8,128)}, f32[2,8,128]{2,1,0:T(8,128)}) custom-call(s32[2,64]{1,0:T(2,128)} %bitcast.7, s32[4]{0:T(128)} %refs_1_.6, f32[4,256]{1,0:T(4,128)} %refs_2_.3, f32[4,256]{1,0:T(4,128)} %refs_3_.1, f32[16,8,128]{2,1,0:T(8,128)} %get-tuple-element.7.refs_4_), custom_call_target="tpu_custom_call" | custom-call | tf_op jit(solution)/shard_map/exchange_sums/pallas_call | solution.py:703
  33.4 7.7 %potential_tiles.1 = (f32[1024,8192]{1,0:T(8,128)}, f32[4,256]{1,0:T(4,128)}, f32[4]{0:T(128)}) custom-call(s32[2,64]{1,0:T(2,128)} %bitcast.8, f32[3,16384]{1,0:T(4,128)} %refs_1_.7, f32[128,128]{1,0:T(8,128)} %bitcast.4, f32[16,8,128]{2,1,0:T(8,128)} %exchange_points.1.refs_4_.refs_3_, ...), custom_call_target="tpu_custom_call", output_to_operand_aliasing={{0}: (6, {})} | custom-call | tf_op jit(solution)/shard_map/potential_tiles/pallas_call | solution.py:734
where the time goes:
time: 41.5 us; the launch traced here: 41 us
  Pallas kernels  40.4 us (97%)
  between operations  0.65 us (2%)
    pallas_call x1, Pallas kernels, local(): pl.pallas_call(lambda *refs: exchange_sums(sizes, *refs), out_shape=(slot...  16.6 us
    pallas_call x1, Pallas kernels, local(): pl.pallas_call(lambda *refs: exchange_points(sizes, *refs), out_shape=slo...  9.1 us
    pallas_call x1, Pallas kernels, local(): pl.pallas_call(lambda *refs: potential_tiles(sizes, fills, *refs), out_sh...  7.68 us
    pallas_call x1, Pallas kernels, local(): pl.pallas_call(lambda *refs: density_tiles(sizes, fills, *refs), out_shap...  6.99 us

commit v1 on v0

--- a/solution.py
+++ b/solution.py
@@ -148,7 +148,9 @@
     own = pltpu.make_async_copy(staged.at[me], out_ref.at[me], own_sem)
     own.start()
     for copy in copies:
-        copy.wait()
+        copy.wait_recv()
+    for copy in copies:
+        copy.wait_send()
     own.wait()
 
 
@@ -220,8 +222,9 @@
         copies.append(copy)
     kept = fetch([(sums_ref.at[me], landed.at[me])], own_sem)
     for copy in copies:
-        copy.wait()
+        copy.wait_recv()
     kept[0].wait()
+    sent = copies
 
     for batch in range(batches):
         total = None
@@ -243,7 +246,8 @@
         copy.start()
         copies.append(copy)
     for copy in copies:
-        copy.wait()
+        copy.wait_recv()
+    sent += copies
     summed = col_sums[0]
     for entry in range(1, col_size):
         summed = summed + col_sums[entry]
@@ -305,7 +309,9 @@
     extra[1] = point_scale * energy
     kept = fetch([(staged.at[me], out_ref.at[me]), (extra, extra_ref)], own_sem)
     for copy in copies:
-        copy.wait()
+        copy.wait_recv()
+    for copy in sent + copies:
+        copy.wait_send()
     for copy in kept:
         copy.wait()
 
@@ -392,8 +398,10 @@
     centres_hbm,
     exponents_hbm,
     points_hbm,
+    sums_hbm,
+    matrix_ref,
     sums_ref,
-    matrix_ref,
+    out_sem,
     points_ref,
     blocks_ref,
     centres_ref,
@@ -492,8 +500,11 @@
         for slot, chosen, piece in results:
             sums_ref[slot] = jnp.where(chosen, piece, sums_ref[slot])
 
+    out = pltpu.make_async_copy(sums_ref, sums_hbm, out_sem)
+    out.start()
     for index in range(fills):
         fill_copy(index).wait()
+    out.wait()
 
 
 def potential_tiles(
@@ -507,8 +518,11 @@
     extra_hbm,
     given_ref,
     matrix_ref,
+    samples_hbm,
+    amounts_hbm,
     samples_ref,
     amounts_ref,
+    out_sem,
     fields_ref,
     extra_ref,
     points_ref,
@@ -577,6 +591,7 @@
                 0, place : place + 1, :
             ]
         amounts_ref[batch] = jnp.sum(extra_ref[1, batch * halves : (batch + 1) * halves, :])
+    outs = fetch([(samples_ref, samples_hbm), (amounts_ref, amounts_hbm)], out_sem)
 
     def one(item):
         tile, half = item_tile[item], item_half[item]
@@ -605,8 +620,6 @@
             goal = jnp.where(GROUP * group + k < items, tile_goal[tile], grid_size)
             total[goal] += result
 
-    for index in every_fill:
-        fill_copy(index).wait()
 
     def tile_copy(tile):
         row = pl.multiple_of((tile_row[tile] - first_row) * BLK, BLK)
@@ -615,17 +628,32 @@
             total.at[tile], matrix_ref.at[pl.ds(row, BLK), pl.ds(column, BLK)], tile_sem.at[tile]
         )
 
-    @pl.loop(0, tiles)
-    def _(tile):
-        @pl.when(tile_goal[tile] == tile)
-        def _():
-            tile_copy(tile).start()
+    def write_rows(first, last):
+        @pl.loop(0, tiles)
+        def _(tile):
+            row = tile_row[tile] - first_row
+
+            @pl.when((tile_goal[tile] == tile) & (row >= first) & (row < last))
+            def _():
+                tile_copy(tile).start()
+
+    per_block = BLK // FILL_ROWS
+    ready = fills // per_block
+    write_rows(0, ready)
+    for block in range(ready, row_blocks):
+        for index in range(max(block * per_block, fills), (block + 1) * per_block):
+            fill_copy(index).wait()
+        if block % 2 == 1 or block == row_blocks - 1:
+            write_rows(max(ready, block - block % 2), block + 1)
 
     @pl.loop(0, tiles)
     def _(tile):
         @pl.when(tile_goal[tile] == tile)
         def _():
             tile_copy(tile).wait()
+
+    for copy in outs:
+        copy.wait()
 
 
 def local(density, centres, exponents, coords, weights, core_density, counts, blocks):
@@ -687,8 +715,10 @@
         lambda *refs: density_tiles(sizes, fills, *refs),
         out_shape=(slots, matrix),
         in_specs=[hbm] * 5,
-        out_specs=(vmem, anywhere),
+        out_specs=(anywhere, anywhere),
         scratch_shapes=[
+            pltpu.VMEM(slot_shape, F32),
+            pltpu.SemaphoreType.DMA,
             *function_memory,
             pltpu.VMEM((grid_size, BLK, BLK), BF16),
             pltpu.VMEM((FILL_ROWS, col_count), F32),
@@ -739,8 +769,11 @@
             jax.ShapeDtypeStruct((batches,), F32),
         ),
         in_specs=[hbm] * 6 + [anywhere],
-        out_specs=(anywhere, vmem, smem),
+        out_specs=(anywhere, anywhere, anywhere),
         scratch_shapes=[
+            pltpu.VMEM((batches, points_len), F32),
+            pltpu.SMEM((batches,), F32),
+            pltpu.SemaphoreType.DMA((2,)),
             pltpu.VMEM(slot_shape, F32),
             pltpu.VMEM((2, batches * halves, BLK), F32),
             *function_memory,

time: 41.5 us -> 41.3 us (level)
    pallas_call x1, Pallas kernels: 7.68 us -> 7.03 us  [local(): pl.pallas_call(lambda *refs: potential_tiles(sizes, fills, *refs), out_sh...]
where the time goes in v1:
time: 41.3 us; the launch traced here: 40.8 us
  Pallas kernels  40.1 us (97%)
  between operations  0.65 us (2%)
    pallas_call x1, Pallas kernels, local(): pl.pallas_call(lambda *refs: exchange_sums(sizes, *refs), out_shape=(slot...  17 us
    pallas_call x1, Pallas kernels, local(): pl.pallas_call(lambda *refs: exchange_points(sizes, *refs), out_shape=slo...  9.11 us
    pallas_call x1, Pallas kernels, local(): pl.pallas_call(lambda *refs: potential_tiles(sizes, fills, *refs), out_sh...  7.03 us
    pallas_call x1, Pallas kernels, local(): pl.pallas_call(lambda *refs: density_tiles(sizes, fills, *refs), out_shap...  6.96 us

profile of v1, /device:TPU:0, one launch (start us, length us, event | category | flops | bytes accessed | tf_op | source)
XLA Modules:
  0.0 40.8 jit_solution(34284978619935498)
XLA Ops:
  0.6 9.1 %exchange_points.1.refs_4_.refs_3_ = f32[16,8,128]{2,1,0:T(8,128)} custom-call(s32[2,64]{1,0:T(2,128)} %bitcast.5, s32[4]{0:T(128)} %refs_1_.6, f32[3,4,256]{2,1,0:T(4,128)} %bitcast.9), custom_call_target="tpu_custom_call" | custom-call | tf_op jit(solution)/shard_map/exchange_points/pallas_call | solution.py:689
  9.8 7.0 %density_tiles.1 = (f32[16,8,128]{2,1,0:T(8,128)}, f32[1024,8192]{1,0:T(8,128)}) custom-call(s32[2,64]{1,0:T(2,128)} %bitcast.6, bf16[1024,8192]{1,0:T(8,128)(2,1)} %refs_1_.5, f32[3,16384]{1,0:T(4,128)} %refs_1_.7, f32[128,128]{1,0:T(8,128)} %bitcast.3, f32[16,8,128]{2,1,0:T(8,128)} %exchange_points.1.refs_4_.refs_3_), custom_call_target="tpu_custom_call" | custom-call | tf_op jit(solution)/shard_map/density_tiles/pallas_call | solution.py:714
  16.7 17.0 %exchange_sums.1 = (f32[16,8,128]{2,1,0:T(8,128)}, f32[2,8,128]{2,1,0:T(8,128)}) custom-call(s32[2,64]{1,0:T(2,128)} %bitcast.7, s32[4]{0:T(128)} %refs_1_.6, f32[4,256]{1,0:T(4,128)} %refs_2_.3, f32[4,256]{1,0:T(4,128)} %refs_3_.1, f32[16,8,128]{2,1,0:T(8,128)} %get-tuple-element.7.refs_4_), custom_call_target="tpu_custom_call" | custom-call | tf_op jit(solution)/shard_map/exchange_sums/pallas_call | solution.py:733
  33.7 7.0 %potential_tiles.1 = (f32[1024,8192]{1,0:T(8,128)}, f32[4,256]{1,0:T(4,128)}, f32[4]{0:T(128)}) custom-call(s32[2,64]{1,0:T(2,128)} %bitcast.8, f32[3,16384]{1,0:T(4,128)} %refs_1_.7, f32[128,128]{1,0:T(8,128)} %bitcast.4, f32[16,8,128]{2,1,0:T(8,128)} %exchange_points.1.refs_4_.refs_3_, ...), custom_call_target="tpu_custom_call", output_to_operand_aliasing={{0}: (6, {})} | custom-call | tf_op jit(solution)/shard_map/potential_tiles/pallas_call | solution.py:764
